TPU v7x, 768 devices: a whole 4x8x12 slice. The times are simulated.
768 devices in a mesh: rep: 64 (over x, y, core), fsdp: 12 (over z).
Axes of the slice: x: 4, y: 8, z: 12, core: 2. Of those that a mesh axis runs over, the one named last changes fastest.
Arguments:
- queries: bfloat16 [98304, 4096], P(('rep', 'fsdp')), may hold values from -18 to 18
- resp_keys: bfloat16 [98304, 512], P(('rep', 'fsdp')), may hold values from -6 to 6
- resp_values: bfloat16 [98304, 512], P(('rep', 'fsdp')), may hold values from -6 to 6
- attn_out: bfloat16 [98304, 4096], P(('rep', 'fsdp')), may hold values from -1.796875 to 1.796875
- out_grad: bfloat16 [98304, 4096], P(('rep', 'fsdp')), may hold values from -24 to 24
- lengths: int32 [768], P(('rep', 'fsdp')), may hold values from 1 to 128, 61440 in all
- prefix_keys: bfloat16 [192, 512], P('fsdp'), may hold values from -18 to 18
- prefix_values: bfloat16 [192, 512], P('fsdp'), may hold values from -6 to 6
Outputs:
- query_grad: bfloat16 [98304, 4096], P(('rep', 'fsdp'))
- key_grad: bfloat16 [98304, 512], P(('rep', 'fsdp'))
- value_grad: bfloat16 [98304, 512], P(('rep', 'fsdp'))
- prefix_key_grad: float32 [192, 512], P('fsdp')
- prefix_value_grad: float32 [192, 512], P('fsdp')
Inputs may be any that keep to these rules, and one draw needn't show every extreme that they name: The largest of lengths is exactly 128.
All inputs are finite; a program needn't handle non-finite values. No bound on the sum of `lengths` on one device may be relied on, other than what follows from the above.
Results may differ from a plain program's by a relative error of at most 0.0078.
Values may be sent and summed in bfloat16 or wider, within the bound.
No kernel may reach another device: no remote copies, remote signals or barrier semaphores. Data moves between devices by JAX's collectives and lax.ppermute only.
A program may use at most 32 MiB of HBM per device.

v0:
```python
import jax
import jax.numpy as jnp
from jax import lax
from jax.sharding import PartitionSpec as P

HEAD_DIM = 128
Q_HEADS = 32
KV_HEADS = 4


masked_fill = -1e30


def laid_out(blocks, dim):
    blocks = jnp.moveaxis(blocks, 0, dim)
    shape = blocks.shape
    return blocks.reshape(*shape[:dim], shape[dim] * shape[dim + 1], *shape[dim + 2 :])


def from_everyone(x, axis):
    peers = lax.axis_size(axis)
    return lax.all_to_all(jnp.broadcast_to(x[None], (peers, *x.shape)), axis, 0, 0, tiled=True)


def gathered_copies(x, axis, dim):
    return laid_out(from_everyone(x, axis), dim)


def side_by_side(arrays, axis, dim, along):
    ends, at = ([], 0)
    for a in arrays[:-1]:
        at += a.shape[along]
        ends.append(at)
    both = jnp.concatenate(arrays, axis=along)
    return tuple(jnp.split(gathered_copies(both, axis, dim), ends, axis=along))


def split_up(x, dim, peers):
    before, after = (x.shape[:dim], x.shape[dim + 1 :])
    return jnp.moveaxis(x.reshape(*before, peers, -1, *after), dim, 0)


def sent_and_summed(x, axis, dim):
    peers = lax.axis_size(axis)
    blocks = lax.all_to_all(split_up(x, dim, peers), axis, 0, 0, tiled=True)
    return jnp.sum(blocks, axis=0)


def sent_together(arrays, axis, dim, along):
    ends, at = ([], 0)
    for a in arrays[:-1]:
        at += a.shape[along]
        ends.append(at)
    both = jnp.concatenate(arrays, axis=along)
    return tuple(jnp.split(sent_and_summed(both, axis, dim), ends, axis=along))


def over_pieces(x, axis):
    blocks = lax.all_gather(x, axis)
    return blocks.sum(axis=0)


def local_grads(
    queries, resp_keys, resp_values, attn_out, out_grad, length, prefix_keys, prefix_values
):
    resp_rows = queries.shape[0]
    prefix_rows = prefix_keys.shape[0]
    key_count = prefix_rows + resp_rows
    all_keys = jnp.concatenate([prefix_keys, resp_keys], axis=0)
    all_values = jnp.concatenate([prefix_values, resp_values], axis=0)
    row_index = jnp.arange(resp_rows, dtype=jnp.int32)[:, None]
    col_index = jnp.arange(key_count, dtype=jnp.int32)[None, :]
    live_rows = row_index < length
    visible = live_rows & ((col_index < prefix_rows) | (col_index - prefix_rows <= row_index))
    dead_rows = 1.0 - live_rows.astype(jnp.float32)
    group_size = Q_HEADS // KV_HEADS
    score_scale = HEAD_DIM ** (-0.5)
    block_width = group_size * HEAD_DIM
    query_parts = []
    key_parts = []
    value_parts = []
    for group_index in range(KV_HEADS):
        lower = group_index * block_width
        q_block = queries[:, lower : lower + block_width].reshape(resp_rows, group_size, HEAD_DIM)
        out_block = attn_out[:, lower : lower + block_width].reshape(
            resp_rows, group_size, HEAD_DIM
        )
        grad_block = out_grad[:, lower : lower + block_width].reshape(
            resp_rows, group_size, HEAD_DIM
        )
        key_block = all_keys[:, group_index * HEAD_DIM : (group_index + 1) * HEAD_DIM]
        value_block = all_values[:, group_index * HEAD_DIM : (group_index + 1) * HEAD_DIM]
        scores = (
            jnp.einsum("rhd,kd->hrk", q_block, key_block, preferred_element_type=jnp.float32)
            * score_scale
        )
        scores = jnp.where(visible[None], scores, masked_fill)
        row_max = jnp.max(scores, axis=2, keepdims=True)
        shifted = jnp.where(visible[None], jnp.exp(scores - row_max), 0.0)
        denominator = jnp.sum(shifted, axis=2, keepdims=True) + dead_rows[None]
        log_total = row_max + jnp.log(denominator)
        attn_prob = jnp.where(visible[None], jnp.exp(scores - log_total), 0.0)
        prob_half = attn_prob.astype(jnp.bfloat16)
        value_part = jnp.einsum(
            "hrk,rhd->kd", prob_half, grad_block, preferred_element_type=jnp.float32
        )
        prob_grad = jnp.einsum(
            "rhd,kd->hrk", grad_block, value_block, preferred_element_type=jnp.float32
        )
        row_delta = jnp.einsum(
            "rhd,rhd->hr", grad_block, out_block, preferred_element_type=jnp.float32
        )
        score_half = (attn_prob * (prob_grad - row_delta[:, :, None])).astype(jnp.bfloat16)
        query_part = (
            jnp.einsum("hrk,kd->rhd", score_half, key_block, preferred_element_type=jnp.float32)
            * score_scale
        )
        key_part = (
            jnp.einsum("hrk,rhd->kd", score_half, q_block, preferred_element_type=jnp.float32)
            * score_scale
        )
        query_parts.append(query_part.reshape(resp_rows, block_width))
        key_parts.append(key_part)
        value_parts.append(value_part)
    query_grad = jnp.concatenate(query_parts, axis=1).astype(jnp.bfloat16)
    key_whole = jnp.concatenate(key_parts, axis=1)
    value_whole = jnp.concatenate(value_parts, axis=1)
    return (query_grad, key_whole, value_whole)


def on_device(
    queries, resp_keys, resp_values, attn_out, out_grad, lengths, prefix_keys, prefix_values
):
    shared_keys, shared_values = side_by_side((prefix_keys, prefix_values), "fsdp", 0, 1)
    query_grad, key_whole, value_whole = local_grads(
        queries, resp_keys, resp_values, attn_out, out_grad, lengths[0], shared_keys, shared_values
    )
    prefix_rows = shared_keys.shape[0]
    prefix_key_part = key_whole[:prefix_rows]
    prefix_value_part = value_whole[:prefix_rows]
    within_keys, within_values = sent_together((prefix_key_part, prefix_value_part), "fsdp", 0, 1)
    key_sums, value_sums = (over_pieces(within_keys, "rep"), over_pieces(within_values, "rep"))
    key_grad = key_whole[prefix_rows:].astype(jnp.bfloat16)
    value_grad = value_whole[prefix_rows:].astype(jnp.bfloat16)
    return (query_grad, key_grad, value_grad, key_sums, value_sums)


def solution(mesh):
    in_specs = (
        P(("rep", "fsdp"), None),
        P(("rep", "fsdp"), None),
        P(("rep", "fsdp"), None),
        P(("rep", "fsdp"), None),
        P(("rep", "fsdp"), None),
        P(("rep", "fsdp")),
        P("fsdp", None),
        P("fsdp", None),
    )
    out_specs = (
        P(("rep", "fsdp"), None),
        P(("rep", "fsdp"), None),
        P(("rep", "fsdp"), None),
        P("fsdp", None),
        P("fsdp", None),
    )
    return jax.shard_map(
        on_device, mesh=mesh, in_specs=in_specs, out_specs=out_specs, check_vma=False
    )
```

profile of v0, /device:TPU:1, one launch (start us, length us, event | category | flops | bytes accessed | tf_op | source)
XLA Modules:
  0.0 277.4 jit_solution(8780044489022661734)
XLA Ops:
  7.2 0.8 pad_maximum_fusion.6
  8.0 0.8 broadcast_in_dim.94
  8.8 15.7 %all-to-all-start = ((bf16[12,16,1024]{2,1,0:T(8,128)(2,1)}), bf16[12,16,1024]{2,1,0:T(8,128)(2,1)}, u32[]{:S(2)}, u32[]{:S(2)}) async-start(bf16[12,16,1024]{2,1,0:T(8,128)(2,1)} %broadcast_in_dim.94), calls=%async_computation | async-start | bytes 786432 | tf_op jit(solution)/shard_map/all_to_all | solution.py:22
  25.2 0.8 fusion.90
  29.8 0.9 fusion.89
  30.7 1.1 copy.118
  31.8 1.1 copy.122
  33.5 1.2 multiply_reduce_fusion
  34.9 1.2 multiply_reduce_fusion.2
  36.4 1.2 multiply_reduce_fusion.1
  38.3 5.0 %all-to-all-done = bf16[12,16,1024]{2,1,0:T(8,128)(2,1)} async-done(((bf16[12,16,1024]{2,1,0:T(8,128)(2,1)}), bf16[12,16,1024]{2,1,0:T(8,128)(2,1)}, u32[]{:S(2)}, u32[]{:S(2)}) %all-to-all-start) | async-done | bytes 393248 | tf_op jit(solution)/shard_map/all_to_all | solution.py:22
  43.3 1.0 fusion.91
  45.8 1.0 select_reduce_fusion.3
  52.5 1.0 pad_maximum_fusion.2
  53.5 1.0 slice.112
  54.6 36.0 %all_to_all.10 = f32[12,16,1024]{2,1,0:T(8,128)} all-to-all(f32[12,16,1024]{2,1,0:T(8,128)S(1)} %bitcast.185), channel_id=1, replica_groups=mesh['rep'=64,'fsdp'=12] {'fsdp'}, dimensions={0} | all-to-all | bytes 1572864 | tf_op jit(solution)/shard_map/all_to_all | solution.py:45
  90.6 1.2 reduce_sum.67
  93.2 1.6 slice.186
  94.8 1.6 slice.187
  98.6 1.0 pad_maximum_fusion
  99.6 78.0 %all-gather.7.cloned.1.call-done = f32[1024,512]{1,0:T(8,128)} async-done(((f32[16,512]{1,0:T(8,128)}), f32[1024,512]{1,0:T(8,128)}) %all-gather.7.cloned.1.call-update) | async-done | bytes 2097168 | tf_op jit(solution)/shard_map/all_gather | solution.py:59
  177.6 2.3 reduce_sum.69
  180.0 88.3 %all-gather.5.cloned.1.call-done = f32[1024,512]{1,0:T(8,128)} async-done(((f32[16,512]{1,0:T(8,128)}), f32[1024,512]{1,0:T(8,128)}) %all-gather.5.cloned.1.call-update) | async-done | bytes 2097168 | tf_op jit(solution)/shard_map/all_gather | solution.py:59
  268.3 2.3 reduce_sum.68
  (81 shorter events, 16.1 us)
Async XLA Ops:
  7.2 18.1 %copy-start.5 = (bf16[128,4096]{1,0:T(8,128)(2,1)S(1)}, bf16[128,4096]{1,0:T(8,128)(2,1)}, u32[]{:S(2)}) copy-start(bf16[128,4096]{1,0:T(8,128)(2,1)} %param.8) | copy-start | bytes 3145732
  8.8 34.5 %all-to-all-start = ((bf16[12,16,1024]{2,1,0:T(8,128)(2,1)}), bf16[12,16,1024]{2,1,0:T(8,128)(2,1)}, u32[]{:S(2)}, u32[]{:S(2)}) async-start(bf16[12,16,1024]{2,1,0:T(8,128)(2,1)} %broadcast_in_dim.94), calls=%async_computation | async-start | bytes 786432 | tf_op jit(solution)/shard_map/all_to_all | solution.py:22
  24.5 153.1 %all-gather.7.cloned.1.call-start = ((), (), s32[]{:S(2)}) async-start(), calls=%async_computation.3 | async-start | bytes 2129920 | tf_op jit(solution)/shard_map/all_gather | solution.py:59
  26.0 0.9 copy-start.8
  26.0 1.4 copy-start.6
  26.2 18.9 %copy-start.1 = (bf16[128,1024]{0,1:T(8,128)(2,1)}, bf16[128,1024]{0,1:T(8,128)(2,1)S(1)}, u32[]{:S(2)}) copy-start(bf16[128,1024]{0,1:T(8,128)(2,1)S(1)} %copy.121) | copy-start | bytes 786436
  27.5 2.3 copy-start.7
  37.5 6.8 %copy-start = (bf16[128,512]{1,0:T(8,128)(2,1)S(1)}, bf16[128,512]{1,0:T(8,128)(2,1)}, u32[]{:S(2)}) copy-start(bf16[128,512]{1,0:T(8,128)(2,1)} %param.9) | copy-start | bytes 393220
  44.4 1.0 copy-start.9
  46.8 0.9 copy-start.4
  50.0 1.0 copy-start.2
  52.5 1.1 copy-start.3
  92.4 175.8 %all-gather.5.cloned.1.call-start = ((), (), s32[]{:S(2)}) async-start(), calls=%async_computation.2 | async-start | bytes 2129920 | tf_op jit(solution)/shard_map/all_gather | solution.py:59
  97.2 0.9 copy-start.10
Sparse Core Ops, SparseCore 0:
  92.5 85.0 all-gather.6
  182.1 86.0 all-gather.4
where the time goes:
time: 278 us; the launch traced here: 277 us
  waiting for transfers between devices  172 us (62%)
  blocking collectives  36 us (13%)
  local copies, waits for them, and re-layouts  17.7 us (6%)
  starting transfers between devices  15.8 us (6%)
  between operations  15.2 us (5%)
  other arithmetic  13.8 us (5%)
  matrix products  7.09 us (3%)
    all_gather x2, waiting for transfers between devices, over_pieces(): blocks = lax.all_gather(x, axis)  166 us
    all_to_all x1, blocking collectives, sent_and_summed(): blocks = lax.all_to_all(split_up(x, dim, peers), axis, 0, 0, tiled=True)  36 us
    all_to_all x1, starting transfers between devices, from_everyone(): lax.all_to_all(jnp.broadcast_to(x[None], (peers, *x.shape)), axis, 0, 0,...  15.7 us
    unnamed x39, local copies, waits for them, and re-layouts  8.5 us
  transfers between devices with their start and end apart: 3, of which 3 were waited for; matrix products, arithmetic and copies ran while one was open for 7% of the time, Pallas kernels for 0%

commit v1 on v0

v1 whole, which is shorter than its diff:
```python
import functools

import jax
import jax.numpy as jnp
from jax import lax
from jax.experimental import pallas as pl
from jax.experimental.pallas import tpu as pltpu
from jax.sharding import Mesh, PartitionSpec as P

HEAD_DIM = 128
Q_HEADS = 32
KV_HEADS = 4
GROUP = Q_HEADS // KV_HEADS
PAIR = 2

bf16 = jnp.bfloat16
f32 = jnp.float32
SCALE = HEAD_DIM ** (-0.5)
LOG2E = 1.4426950408889634
masked_fill = -1e30


def dot(a, b, ca, cb):
    return lax.dot_general(a, b, (((ca,), (cb,)), ((), ())), preferred_element_type=f32)


def grads_kernel(
    meta, q_ref, do_ref, o_ref, k_ref, v_ref, pk_ref, pv_ref,
    dq_ref, dk_ref, dv_ref, pdk_ref, pdv_ref, p_s, s_s,
):
    rows = q_ref.shape[0]
    prefix = pk_ref.shape[0]
    length = meta[0]
    keys = jnp.concatenate([pk_ref[...], k_ref[...]], axis=0)
    values = jnp.concatenate([pv_ref[...], v_ref[...]], axis=0)
    key_count = prefix + rows
    eye = (
        lax.broadcasted_iota(jnp.int32, (HEAD_DIM, HEAD_DIM), 0)
        == lax.broadcasted_iota(jnp.int32, (HEAD_DIM, HEAD_DIM), 1)
    ).astype(f32).astype(bf16)
    keys_t = dot(eye, keys, 1, 1).astype(bf16)
    wide = PAIR * rows
    time = lax.broadcasted_iota(jnp.int32, (1, wide), 1) % rows
    live = time < length
    own = lax.broadcasted_iota(jnp.int32, (rows, wide), 0)
    causal = own <= lax.broadcasted_iota(jnp.int32, (rows, wide), 1) % rows
    ones = jnp.ones((8, 2 * HEAD_DIM), bf16)

    def stacked(ref, first, count):
        return jnp.concatenate(
            [ref[:, h * HEAD_DIM : (h + 1) * HEAD_DIM] for h in range(first, first + count)], axis=0
        )

    for pair in range(GROUP // PAIR):
        first = pair * PAIR
        q = stacked(q_ref, first, PAIR)
        grad = stacked(do_ref, first, PAIR)
        out = stacked(o_ref, first, PAIR)
        prod = grad.astype(f32) * out.astype(f32)
        high = prod.astype(bf16)
        low = (prod - high.astype(f32)).astype(bf16)
        delta = dot(ones, jnp.concatenate([high, low], axis=1), 1, 1)[0:1]
        scores = dot(keys, q, 1, 1)
        s_p = scores[:prefix]
        s_r = jnp.where(causal, scores[prefix:], masked_fill)
        top = jnp.maximum(
            jnp.max(s_p, axis=0, keepdims=True), jnp.max(s_r, axis=0, keepdims=True)
        )
        e_p = jnp.exp2((s_p - top) * (SCALE * LOG2E))
        e_r = jnp.exp2((s_r - top) * (SCALE * LOG2E))
        total = jnp.sum(e_p, axis=0, keepdims=True) + jnp.sum(e_r, axis=0, keepdims=True)
        weight = jnp.where(live, 1.0 / total, 0.0)
        prob = jnp.concatenate([e_p, e_r], axis=0) * weight
        prob_grad = dot(values, grad, 1, 1)
        score_half = (prob * (prob_grad - delta)).astype(bf16)
        p_s[:, first * rows : (first + PAIR) * rows] = prob.astype(bf16)
        s_s[:, first * rows : (first + PAIR) * rows] = score_half
        dq_t = dot(keys_t, score_half, 1, 0) * SCALE
        for i in range(PAIR):
            lo = (first + i) * HEAD_DIM
            dq_ref[:, lo : lo + HEAD_DIM] = dq_t[:, i * rows : (i + 1) * rows].T.astype(bf16)
    dv = dot(p_s[...], stacked(do_ref, 0, GROUP), 1, 0)
    dk = dot(s_s[...], stacked(q_ref, 0, GROUP), 1, 0) * SCALE
    dk_ref[...] = dk[prefix:].astype(bf16)
    dv_ref[...] = dv[prefix:].astype(bf16)
    pdk_ref[...] = dk[:prefix]
    pdv_ref[...] = dv[:prefix]


def local_grads(length, queries, out_grad, attn_out, keys, values, prefix_keys, prefix_values):
    rows = queries.shape[0]
    prefix = prefix_keys.shape[0]
    block = GROUP * HEAD_DIM
    wide = pl.BlockSpec((rows, block), lambda g, m: (0, g))
    slim = pl.BlockSpec((rows, HEAD_DIM), lambda g, m: (0, g))
    pre = pl.BlockSpec((prefix, HEAD_DIM), lambda g, m: (0, g))
    return pl.pallas_call(
        grads_kernel,
        grid_spec=pltpu.PrefetchScalarGridSpec(
            num_scalar_prefetch=1,
            grid=(KV_HEADS,),
            in_specs=[wide, wide, wide, slim, slim, pre, pre],
            out_specs=[wide, slim, slim, pre, pre],
            scratch_shapes=[
                pltpu.VMEM((prefix + rows, GROUP * rows), bf16),
                pltpu.VMEM((prefix + rows, GROUP * rows), bf16),
            ],
        ),
        out_shape=[
            jax.ShapeDtypeStruct((rows, Q_HEADS * HEAD_DIM), bf16),
            jax.ShapeDtypeStruct((rows, KV_HEADS * HEAD_DIM), bf16),
            jax.ShapeDtypeStruct((rows, KV_HEADS * HEAD_DIM), bf16),
            jax.ShapeDtypeStruct((prefix, KV_HEADS * HEAD_DIM), f32),
            jax.ShapeDtypeStruct((prefix, KV_HEADS * HEAD_DIM), f32),
        ],
        compiler_params=pltpu.CompilerParams(vmem_limit_bytes=32 * 1024 * 1024),
        name="grads",
    )(length, queries, out_grad, attn_out, keys, values, prefix_keys, prefix_values)


def exchanged(x, axes):
    return lax.all_to_all(x, axes, 0, 0, tiled=True)


def on_device(
    queries, resp_keys, resp_values, attn_out, out_grad, lengths, prefix_keys, prefix_values
):
    core = lax.axis_index("core")
    n_x, n_y, n_z = lax.axis_size("x"), lax.axis_size("y"), lax.axis_size("z")
    part = prefix_keys.shape[0]
    width = prefix_keys.shape[1]
    mine = jnp.where(core == 0, prefix_keys, prefix_values)
    rows = exchanged(jnp.broadcast_to(mine[None], (n_z, part, width)), "z")
    both = lax.all_gather(rows.reshape(n_z * part, width), "core")
    query_grad, key_grad, value_grad, pre_k, pre_v = local_grads(
        lengths, queries, out_grad, attn_out, resp_keys, resp_values, both[0], both[1]
    )
    theirs = jnp.where(core == 0, pre_v, pre_k).astype(bf16)
    keep = jnp.where(core == 0, pre_k, pre_v)
    got = lax.ppermute(theirs, "core", [(0, 1), (1, 0)])
    chip = (keep + got.astype(f32)).astype(bf16)
    cols = width // n_x
    blocks = chip.reshape(n_z, part, n_x, cols).transpose(2, 0, 1, 3).reshape(n_x * n_z, part, cols)
    summed = jnp.sum(exchanged(blocks, ("x", "z")).astype(f32), axis=0)
    spread = exchanged(jnp.broadcast_to(summed[None], (n_x * n_y, part, cols)), ("x", "y"))
    whole = jnp.sum(spread.reshape(n_x, n_y, part, cols), axis=1)
    whole = whole.transpose(1, 0, 2).reshape(part, width)
    final = lax.all_gather(whole, "core")
    return (query_grad, key_grad, value_grad, final[0], final[1])


def solution(mesh):
    n_rep, n_z = mesh.devices.shape
    n_y = 8
    chips = Mesh(mesh.devices.reshape(n_rep // (2 * n_y), n_y, 2, n_z), ("x", "y", "core", "z"))
    rep = ("x", "y", "core")
    rows = P((*rep, "z"), None)
    in_specs = (rows, rows, rows, rows, rows, P((*rep, "z")), P("z", None), P("z", None))
    out_specs = (rows, rows, rows, P("z", None), P("z", None))
    return jax.shard_map(
        on_device, mesh=chips, in_specs=in_specs, out_specs=out_specs, check_vma=False
    )
```

time: 278 us -> 95.2 us (0.34)
  waiting for transfers between devices: 172 us -> 12.7 us
  between operations: 15.2 us -> 1.38 us
  local copies, waits for them, and re-layouts: 17.7 us -> 4.86 us
  other arithmetic: 13.8 us -> 1.04 us
  blocking collectives: 36 us -> 48 us
  Pallas kernels: 0 us -> 8.83 us
  matrix products: 7.09 us -> 0 us
    all_gather x2 -> x0, waiting for transfers between devices: 166 us -> none  [over_pieces(): blocks = lax.all_gather(x, axis)]
    all_gather x0 -> x2, blocking collectives: none -> 10.2 us  [the longest x1 5.83 us: on_device(): final = lax.all_gather(whole, 'core')]
    pallas_call x0 -> x1, Pallas kernels: none -> 8.83 us  [local_grads(): pl.pallas_call(grads_kernel, grid_spec=pltpu.PrefetchScalarGridSpec(num_s...]
    dot_general x20 -> x0, matrix products: 7.09 us -> none  [the longest x4 1.76 us: local_grads(): jnp.einsum('rhd,kd->hrk', grad_block, value_block, preferred_element_type...]
    reduce_sum x4 -> x2, other arithmetic: 6.88 us -> 0.07 us  [the longest x1 0.05 us: on_device(): summed = jnp.sum(exchanged(blocks, ('x', 'z')).astype(f32), axis=0)]
    all_to_all x1, waiting for transfers between devices: 4.98 us -> 11.6 us  [exchanged(): return lax.all_to_all(x, axes, 0, 0, tiled=True)]
    slice x6 -> x0, local copies, waits for them, and re-layouts: 5.93 us -> none  [the longest x1 1.62 us: on_device(): value_grad = value_whole[prefix_rows:].astype(jnp.bfloat16)]
    unnamed x39 -> x10, local copies, waits for them, and re-layouts: 8.5 us -> 3.38 us
  transfers between devices with their start and end apart: 3 -> 2, of which waited for: 3 -> 2; matrix products, arithmetic and copies ran while one was open for 7% -> 0% of each run, Pallas kernels for 0% -> 0%
where the time goes in v1:
time: 95.2 us; the launch traced here: 94.7 us
  blocking collectives  48 us (50%)
  starting transfers between devices  18 us (19%)
  waiting for transfers between devices  12.7 us (13%)
  Pallas kernels  8.83 us (9%)
  local copies, waits for them, and re-layouts  4.86 us (5%)
  between operations  1.38 us (1%)
  other arithmetic  1.04 us (1%)
    all_to_all x2, blocking collectives, exchanged(): return lax.all_to_all(x, axes, 0, 0, tiled=True)  37.8 us
    all_to_all x1, starting transfers between devices, exchanged(): return lax.all_to_all(x, axes, 0, 0, tiled=True)  15.7 us
    all_to_all x1, waiting for transfers between devices, exchanged(): return lax.all_to_all(x, axes, 0, 0, tiled=True)  11.6 us
    pallas_call x1, Pallas kernels, local_grads(): pl.pallas_call(grads_kernel, grid_spec=pltpu.PrefetchScalarGridSpec(num_s...  8.83 us
    all_gather x1, blocking collectives, on_device(): final = lax.all_gather(whole, 'core')  5.83 us
    all_gather x1, blocking collectives, on_device(): both = lax.all_gather(rows.reshape(n_z * part, width), 'core')  4.35 us
    unnamed x10, local copies, waits for them, and re-layouts  3.38 us
    ppermute x1, starting transfers between devices, on_device(): got = lax.ppermute(theirs, 'core', [(0, 1), (1, 0)])  2.28 us
  transfers between devices with their start and end apart: 2, of which 2 were waited for; matrix products, arithmetic and copies ran while one was open for 0% of the time, Pallas kernels for 0%

profile of v1, /device:TPU:1, one launch (start us, length us, event | category | flops | bytes accessed | tf_op | source)
XLA Modules:
  0.0 94.7 jit_solution(6439121188514308968)
XLA Ops:
  0.6 0.0 copy-start
  0.6 0.8 broadcast_select_fusion
  1.5 0.7 broadcast_in_dim.4
  2.2 15.7 %all-to-all-start = ((bf16[12,16,512]{2,1,0:T(8,128)(2,1)}), bf16[12,16,512]{2,1,0:T(8,128)(2,1)S(1)}, u32[]{:S(2)}, u32[]{:S(2)}) async-start(bf16[12,16,512]{2,1,0:T(8,128)(2,1)} %broadcast_in_dim.4), calls=%async_computation | async-start | bytes 393216 | tf_op jit(solution)/shard_map/all_to_all | solution.py:122
  18.5 11.6 %all-to-all-done = bf16[12,16,512]{2,1,0:T(8,128)(2,1)S(1)} async-done(((bf16[12,16,512]{2,1,0:T(8,128)(2,1)}), bf16[12,16,512]{2,1,0:T(8,128)(2,1)S(1)}, u32[]{:S(2)}, u32[]{:S(2)}) %all-to-all-start) | async-done | bytes 196640 | tf_op jit(solution)/shard_map/all_to_all | solution.py:122
  30.1 4.4 %all_gather.6 = bf16[2,192,512]{2,1,0:T(8,128)(2,1)S(1)} all-gather(bf16[1,192,512]{2,1,0:T(8,128)(2,1)S(1)} %bitcast.16), channel_id=1, replica_groups=mesh['x'=4,'y'=8,'core'=2,'z'=12] {'core'}, dimensions={0}, use_global_device_ids=true | all-gather | bytes 589824 | tf_op jit(solution)/shard_map/all_gather | solution.py:134
  34.5 0.0 copy-start.3
  34.5 0.0 copy-start.4
  34.5 0.0 copy-done
  34.5 0.9 copy-done.3
  35.4 0.1 copy-done.4
  35.5 1.2 %copy-done.1 = bf16[128,4096]{1,0:T(8,128)(2,1)S(1)} copy-done((bf16[128,4096]{1,0:T(8,128)(2,1)S(1)}, bf16[128,4096]{1,0:T(8,128)(2,1)}, u32[]{:S(2)}) %copy-start.1) | copy-done | bytes 1048600
  36.7 1.2 %copy-done.2 = bf16[128,4096]{1,0:T(8,128)(2,1)S(1)} copy-done((bf16[128,4096]{1,0:T(8,128)(2,1)S(1)}, bf16[128,4096]{1,0:T(8,128)(2,1)}, u32[]{:S(2)}) %copy-start.2) | copy-done | bytes 1048600
  37.9 8.8 %grads.1 = (bf16[128,4096]{1,0:T(8,128)(2,1)}, bf16[128,512]{1,0:T(8,128)(2,1)}, bf16[128,512]{1,0:T(8,128)(2,1)}, f32[192,512]{1,0:T(8,128)S(1)}, f32[192,512]{1,0:T(8,128)S(1)}) custom-call(s32[1]{0:T(128)S(6)} %copy.18.meta, bf16[128,4096]{1,0:T(8,128)(2,1)S(1)} %copy-done, bf16[128,4096]{1,0:T(8,128)(2,1)S(1)} %copy-done.1, ...), custom_call_target="tpu_custom_call" | custom-call | tf_op jit(solution)/shard_map/grads/pallas_call | solution.py:97
  46.7 0.1 select_convert_fusion
  46.8 2.3 %collective-permute-start = (bf16[192,512]{1,0:T(8,128)(2,1)S(1)}, bf16[192,512]{1,0:T(8,128)(2,1)S(1)}, u32[]{:S(2)}, u32[]{:S(2)}) collective-permute-start(bf16[192,512]{1,0:T(8,128)(2,1)S(1)} %select_convert_fusion), channel_id=1, source_target_pairs={{0,12},{12,0},{1,13},{13,1},{2,14},{14,2},{3,15},{15,3},{4,16},{16... | collective-permute-start | bytes 589832 | tf_op jit(solution)/shard_map/ppermute | solution.py:140
  49.1 1.0 %collective-permute-done = bf16[192,512]{1,0:T(8,128)(2,1)S(1)} collective-permute-done((bf16[192,512]{1,0:T(8,128)(2,1)S(1)}, bf16[192,512]{1,0:T(8,128)(2,1)S(1)}, u32[]{:S(2)}, u32[]{:S(2)}) %collective-permute-start) | collective-permute-done | bytes 196640 | tf_op jit(solution)/shard_map/ppermute | solution.py:140
  50.1 0.1 add_convert_fusion
  50.2 0.1 reshape.21
  50.3 20.0 %all_to_all.15 = bf16[48,16,128]{2,1,0:T(8,128)(2,1)S(1)} all-to-all(bf16[48,16,128]{2,1,0:T(8,128)(2,1)S(1)} %bitcast.15), channel_id=1, replica_groups=mesh['x'=4,'y'=8,'core'=2,'z'=12] {'x','z'}, dimensions={0} | all-to-all | bytes 393216 | tf_op jit(solution)/shard_map/all_to_all | solution.py:122
  70.3 0.1 convert_reduce_fusion
  70.4 17.8 %all_to_all.16 = f32[32,16,128]{2,1,0:T(8,128)S(1)} all-to-all(f32[32,16,128]{2,1,0:T(8,128)S(1)} %broadcast_in_dim.5), channel_id=1, replica_groups=mesh['x'=4,'y'=8,'core'=2,'z'=12] {'x','y'}, dimensions={0} | all-to-all | bytes 524288 | tf_op jit(solution)/shard_map/all_to_all | solution.py:122
  88.3 5.8 %all_gather.7 = f32[2,16,512]{2,1,0:T(8,128)S(1)} all-gather(f32[1,16,512]{2,1,0:T(8,128)S(1)} %all_gather_reshape.7), channel_id=1, replica_groups=mesh['x'=4,'y'=8,'core'=2,'z'=12] {'core'}, dimensions={0}, use_global_device_ids=true | all-gather | bytes 98304 | tf_op jit(solution)/shard_map/all_gather | solution.py:148
  94.1 0.6 slice_bitcast_fusion.2
  (8 shorter events, 0.1 us)
Async XLA Ops:
  0.6 33.9 %copy-start = (bf16[128,4096]{1,0:T(8,128)(2,1)S(1)}, bf16[128,4096]{1,0:T(8,128)(2,1)}, u32[]{:S(2)}) copy-start(bf16[128,4096]{1,0:T(8,128)(2,1)} %q_ref.1) | copy-start | bytes 3145732
  2.2 28.0 %all-to-all-start = ((bf16[12,16,512]{2,1,0:T(8,128)(2,1)}), bf16[12,16,512]{2,1,0:T(8,128)(2,1)S(1)}, u32[]{:S(2)}, u32[]{:S(2)}) async-start(bf16[12,16,512]{2,1,0:T(8,128)(2,1)} %broadcast_in_dim.4), calls=%async_computation | async-start | bytes 393216 | tf_op jit(solution)/shard_map/all_to_all | solution.py:122
  34.5 0.9 copy-start.3
  34.5 1.0 %copy-start.4 = (bf16[128,512]{1,0:T(8,128)(2,1)S(1)}, bf16[128,512]{1,0:T(8,128)(2,1)}, u32[]{:S(2)}) copy-start(bf16[128,512]{1,0:T(8,128)(2,1)} %v_ref.1) | copy-start | bytes 393220
  35.5 1.2 %copy-start.1 = (bf16[128,4096]{1,0:T(8,128)(2,1)S(1)}, bf16[128,4096]{1,0:T(8,128)(2,1)}, u32[]{:S(2)}) copy-start(bf16[128,4096]{1,0:T(8,128)(2,1)} %do_ref.1) | copy-start | bytes 3145732
  36.7 1.2 %copy-start.2 = (bf16[128,4096]{1,0:T(8,128)(2,1)S(1)}, bf16[128,4096]{1,0:T(8,128)(2,1)}, u32[]{:S(2)}) copy-start(bf16[128,4096]{1,0:T(8,128)(2,1)} %o_ref.1) | copy-start | bytes 3145732
  46.8 3.3 %collective-permute-start = (bf16[192,512]{1,0:T(8,128)(2,1)S(1)}, bf16[192,512]{1,0:T(8,128)(2,1)S(1)}, u32[]{:S(2)}, u32[]{:S(2)}) collective-permute-start(bf16[192,512]{1,0:T(8,128)(2,1)S(1)} %select_convert_fusion), channel_id=1, source_target_pairs={{0,12},{12,0},{1,13},{13,1},{2,14},{14,2},{3,15},{15,3},{4,16},{16... | collective-permute-start | bytes 589832 | tf_op jit(solution)/shard_map/ppermute | solution.py:140

commit v2 on v1

v2 whole, which is shorter than its diff:
```python
import jax
import jax.numpy as jnp
from jax import lax
from jax.experimental import pallas as pl
from jax.experimental.pallas import tpu as pltpu
from jax.sharding import Mesh, PartitionSpec as P

HEAD_DIM = 128
Q_HEADS = 32
KV_HEADS = 4
GROUP = Q_HEADS // KV_HEADS
PAIR = 2
BLOCK = GROUP * HEAD_DIM

bf16 = jnp.bfloat16
f32 = jnp.float32
SCALE = HEAD_DIM ** (-0.5)
EXP2_SCALE = SCALE * 1.4426950408889634
masked_fill = -1e30
VMEM_LIMIT = 24 * 1024 * 1024


def dot(a, b, ca, cb):
    return lax.dot_general(a, b, (((ca,), (cb,)), ((), ())), preferred_element_type=f32)


def stacked(ref, first, count):
    return jnp.concatenate(
        [ref[:, h * HEAD_DIM : (h + 1) * HEAD_DIM] for h in range(first, first + count)], axis=0
    )


def transposed(x):
    side = lax.broadcasted_iota(jnp.int32, (HEAD_DIM, HEAD_DIM), 0)
    eye = (side == lax.broadcasted_iota(jnp.int32, (HEAD_DIM, HEAD_DIM), 1)).astype(f32).astype(bf16)
    return dot(eye, x, 1, 1).astype(bf16)


def own_kernel(q_ref, do_ref, o_ref, k_ref, v_ref, e_ref, g_ref, stat_ref):
    rows = q_ref.shape[0]
    wide = PAIR * rows
    keys, values = k_ref[...], v_ref[...]
    causal = (
        lax.broadcasted_iota(jnp.int32, (rows, wide), 0)
        <= lax.broadcasted_iota(jnp.int32, (rows, wide), 1) % rows
    )
    ones = jnp.ones((8, 2 * HEAD_DIM), bf16)
    for first in range(0, GROUP, PAIR):
        cols = slice(first * rows, (first + PAIR) * rows)
        q, grad, out = (stacked(r, first, PAIR) for r in (q_ref, do_ref, o_ref))
        prod = grad.astype(f32) * out.astype(f32)
        high = prod.astype(bf16)
        low = (prod - high.astype(f32)).astype(bf16)
        delta = dot(ones, jnp.concatenate([high, low], axis=1), 1, 1)
        scores = jnp.where(causal, dot(keys, q, 1, 1), masked_fill)
        top = jnp.max(scores, axis=0, keepdims=True)
        e = jnp.exp2((scores - top) * EXP2_SCALE)
        e_ref[:, cols] = e
        g_ref[:, cols] = e * (dot(values, grad, 1, 1) - delta[0:1])
        stat_ref[0:8, cols] = jnp.broadcast_to(top, (8, wide))
        stat_ref[8:16, cols] = jnp.broadcast_to(jnp.sum(e, axis=0, keepdims=True), (8, wide))
        stat_ref[16:24, cols] = delta


def prefix_kernel(
    meta, q_ref, do_ref, shared_ref, stat_ref, s_out, w_ref, sums_ref, p_s, s_ref, sems
):
    rows = q_ref.shape[0]
    wide = PAIR * rows
    live = lax.broadcasted_iota(jnp.int32, (1, wide), 1) % rows < meta[0]
    copies = []
    for group in range(KV_HEADS):
        slim = slice(group * HEAD_DIM, (group + 1) * HEAD_DIM)
        keys, values = shared_ref[0, :, slim], shared_ref[1, :, slim]
        for first in range(group * GROUP, (group + 1) * GROUP, PAIR):
            cols = slice(first * rows, (first + PAIR) * rows)
            q, grad = (stacked(r, first, PAIR) for r in (q_ref, do_ref))
            own_top, own_sum = stat_ref[0:1, cols], stat_ref[8:9, cols]
            delta = stat_ref[16:17, cols]
            scores = dot(keys, q, 1, 1)
            top = jnp.maximum(jnp.max(scores, axis=0, keepdims=True), own_top)
            e = jnp.exp2((scores - top) * EXP2_SCALE)
            own = jnp.exp2((own_top - top) * EXP2_SCALE)
            total = jnp.sum(e, axis=0, keepdims=True) + own_sum * own
            weight = jnp.where(live, 1.0 / total, 0.0)
            prob = e * weight
            p_s[:, cols] = prob.astype(bf16)
            s_ref[:, cols] = (prob * (dot(values, grad, 1, 1) - delta)).astype(bf16)
            w_ref[:, cols] = jnp.broadcast_to(own * weight, (8, wide))
        cols = slice(group * GROUP * rows, (group + 1) * GROUP * rows)
        copies.append(
            pltpu.make_async_copy(s_ref.at[:, cols], s_out.at[:, cols], sems.at[group])
        )
        copies[-1].start()
        q, grad = (stacked(r, group * GROUP, GROUP) for r in (q_ref, do_ref))
        sums_ref[1, :, slim] = dot(p_s[:, cols], grad, 1, 0).astype(bf16)
        sums_ref[0, :, slim] = (dot(s_ref[:, cols], q, 1, 0) * SCALE).astype(bf16)
    for copy in copies:
        copy.wait()


def rest_kernel(
    q_ref, do_ref, k_ref, pk_ref, e_ref, g_ref, s_ref, w_ref, dq_ref, dk_ref, dv_ref, p_s, s_s
):
    rows = q_ref.shape[0]
    keys_t, prefix_t = transposed(k_ref[...]), transposed(pk_ref[0])
    for first in range(0, GROUP, PAIR):
        cols = slice(first * rows, (first + PAIR) * rows)
        weight = w_ref[0:1, cols]
        p_s[:, cols] = (e_ref[:, cols] * weight).astype(bf16)
        score_half = (g_ref[:, cols] * weight).astype(bf16)
        s_s[:, cols] = score_half
        dq_t = (dot(prefix_t, s_ref[:, cols], 1, 0) + dot(keys_t, score_half, 1, 0)) * SCALE
        for i in range(PAIR):
            lo = (first + i) * HEAD_DIM
            dq_ref[:, lo : lo + HEAD_DIM] = dq_t[:, i * rows : (i + 1) * rows].T.astype(bf16)
    dv_ref[...] = dot(p_s[...], stacked(do_ref, 0, GROUP), 1, 0).astype(bf16)
    dk_ref[...] = (dot(s_s[...], stacked(q_ref, 0, GROUP), 1, 0) * SCALE).astype(bf16)


def columns(rows, width):
    return pl.BlockSpec((rows, width), lambda g, *_: (0, g))


def prefix_columns(which, rows):
    return pl.BlockSpec((1, rows, HEAD_DIM), lambda g, *_: (which, 0, g))


def shape(rows, width, dtype):
    return pltpu.HBM((rows, width), dtype)


def held(*sizes):
    return pltpu.VMEM(sizes[:-1], sizes[-1])


def hbm(*arrays):
    return [pltpu.with_memory_space_constraint(a, pltpu.HBM) for a in arrays]


def vmem(*arrays):
    return [pltpu.with_memory_space_constraint(a, pltpu.VMEM) for a in arrays]


def call(kernel, name, scalars, in_specs, out_specs, out_shape, scratch, flops, moved):
    return pl.pallas_call(
        kernel,
        grid_spec=pltpu.PrefetchScalarGridSpec(
            num_scalar_prefetch=scalars,
            grid=(KV_HEADS,),
            in_specs=in_specs,
            out_specs=out_specs,
            scratch_shapes=scratch,
        ),
        out_shape=out_shape,
        compiler_params=pltpu.CompilerParams(vmem_limit_bytes=VMEM_LIMIT),
        cost_estimate=pl.CostEstimate(flops=flops, bytes_accessed=moved, transcendentals=0),
        name=name,
    )


def own_part(queries, out_grad, attn_out, keys, values):
    rows = queries.shape[0]
    wide, slim = columns(rows, BLOCK), columns(rows, HEAD_DIM)
    total = Q_HEADS * rows
    return call(
        own_kernel, "own_part", 0,
        [wide, wide, wide, slim, slim],
        [columns(rows, GROUP * rows), columns(rows, GROUP * rows), columns(24, GROUP * rows)],
        [shape(rows, total, f32), shape(rows, total, f32), held(24, total, f32)],
        [], 1 << 29, 8 << 20,
    )(*hbm(queries, out_grad, attn_out, keys, values))


def prefix_part(length, queries, out_grad, shared, stats):
    rows, prefix = queries.shape[0], shared.shape[1]
    total = Q_HEADS * rows
    whole = pl.BlockSpec(memory_space=pltpu.VMEM)
    return pl.pallas_call(
        prefix_kernel,
        in_specs=[pl.BlockSpec(memory_space=pltpu.SMEM), whole, whole, whole, whole],
        out_specs=[pl.BlockSpec(memory_space=pltpu.HBM), whole, whole],
        out_shape=[
            shape(prefix, total, bf16), held(8, total, f32),
            held(2, prefix, KV_HEADS * HEAD_DIM, bf16),
        ],
        scratch_shapes=[
            pltpu.VMEM((prefix, total), bf16), pltpu.VMEM((prefix, total), bf16),
            pltpu.SemaphoreType.DMA((KV_HEADS,)),
        ],
        compiler_params=pltpu.CompilerParams(vmem_limit_bytes=VMEM_LIMIT),
        cost_estimate=pl.CostEstimate(flops=1 << 30, bytes_accessed=5 << 20, transcendentals=0),
        name="prefix_part",
    )(length, *vmem(queries, out_grad, shared, stats))


def rest_part(queries, out_grad, keys, shared, e, g, score_half, weight):
    rows, prefix = queries.shape[0], shared.shape[1]
    wide, slim = columns(rows, BLOCK), columns(rows, HEAD_DIM)
    heads = columns(rows, GROUP * rows)
    return call(
        rest_kernel, "rest_part", 0,
        [
            wide, wide, slim, prefix_columns(0, prefix), heads, heads,
            columns(prefix, GROUP * rows), columns(8, GROUP * rows),
        ],
        [wide, slim, slim],
        [
            shape(rows, Q_HEADS * HEAD_DIM, bf16), shape(rows, KV_HEADS * HEAD_DIM, bf16),
            shape(rows, KV_HEADS * HEAD_DIM, bf16),
        ],
        [pltpu.VMEM((rows, GROUP * rows), bf16), pltpu.VMEM((rows, GROUP * rows), bf16)],
        1 << 29, 9 << 20,
    )(*vmem(queries, out_grad), *hbm(keys), shared, *hbm(e, g, score_half), weight)


def exchanged(x, axes):
    return lax.all_to_all(x, axes, 0, 0, tiled=True)


def on_device(
    queries, resp_keys, resp_values, attn_out, out_grad, lengths, prefix_keys, prefix_values
):
    core = lax.axis_index("core")
    n_x, n_y, n_z = lax.axis_size("x"), lax.axis_size("y"), lax.axis_size("z")
    part, width = prefix_keys.shape
    mine = jnp.where(core == 0, prefix_keys, prefix_values)
    rows = exchanged(jnp.broadcast_to(mine[None], (n_z, part, width)), "z")
    e, g, stats = own_part(queries, out_grad, attn_out, resp_keys, resp_values)
    shared = lax.all_gather(rows.reshape(n_z * part, width), "core")
    score_half, weight, sums = prefix_part(lengths, queries, out_grad, shared, stats)
    both = lax.all_gather(sums, "core")
    halves = [jnp.where(core == 0, both[i, 0], both[i, 1]).astype(f32) for i in range(2)]
    chip = (halves[0] + halves[1]).astype(bf16)
    chip, score_half = lax.optimization_barrier((chip, score_half))
    cols = width // n_x
    blocks = chip.reshape(n_z, part, n_x, cols).transpose(2, 0, 1, 3).reshape(n_x * n_z, part, cols)
    blocks = exchanged(blocks, ("x", "z"))
    query_grad, key_grad, value_grad = rest_part(
        queries, out_grad, resp_keys, shared, e, g, score_half, weight
    )
    summed = jnp.sum(blocks.astype(f32), axis=0).astype(bf16)
    spread = exchanged(jnp.broadcast_to(summed[None], (n_x * n_y, part, cols)), ("x", "y"))
    whole = jnp.sum(spread.reshape(n_x, n_y, part, cols).astype(f32), axis=1)
    final = lax.all_gather(whole.transpose(1, 0, 2).reshape(part, width), "core")
    return (query_grad, key_grad, value_grad, final[0], final[1])


def solution(mesh):
    n_rep, n_z = mesh.devices.shape
    n_y = 8
    chips = Mesh(mesh.devices.reshape(n_rep // (2 * n_y), n_y, 2, n_z), ("x", "y", "core", "z"))
    rep = ("x", "y", "core")
    rows = P((*rep, "z"), None)
    in_specs = (rows, rows, rows, rows, rows, P((*rep, "z")), P("z", None), P("z", None))
    out_specs = (rows, rows, rows, P("z", None), P("z", None))
    return jax.shard_map(
        on_device, mesh=chips, in_specs=in_specs, out_specs=out_specs, check_vma=False
    )
```

time: 95.2 us -> 85.4 us (0.90)
  blocking collectives: 48 us -> 32.5 us
  starting transfers between devices: 18 us -> 24 us
  Pallas kernels: 8.83 us -> 14.3 us
  waiting for transfers between devices: 12.7 us -> 9.63 us
  local copies, waits for them, and re-layouts: 4.86 us -> 2.14 us
    all_to_all x2 -> x1, blocking collectives: 37.8 us -> 20 us  [exchanged(): return lax.all_to_all(x, axes, 0, 0, tiled=True)]
    all_to_all x1 -> x2, starting transfers between devices: 15.7 us -> 24 us  [exchanged(): return lax.all_to_all(x, axes, 0, 0, tiled=True)]
    pallas_call x1 -> x3, Pallas kernels: 8.83 us -> 14.3 us  [the longest x1 5.52 us: rest_part(): call(rest_kernel, 'rest_part', 0, [wide, wide, slim, prefix_columns(0, pr...]
    unnamed x10 -> x4, local copies, waits for them, and re-layouts: 3.38 us -> 0.01 us
    all_gather x2 -> x3, blocking collectives: 10.2 us -> 12.5 us  [the longest x1 5.77 us: on_device(): lax.all_gather(whole.transpose(1, 0, 2).reshape(part, width), 'core')]
    ppermute x1 -> x0, starting transfers between devices: 2.28 us -> none  [on_device(): got = lax.ppermute(theirs, 'core', [(0, 1), (1, 0)])]
    all_to_all x1 -> x2, waiting for transfers between devices: 11.6 us -> 9.63 us  [exchanged(): return lax.all_to_all(x, axes, 0, 0, tiled=True)]
    ppermute x1 -> x0, waiting for transfers between devices: 1.05 us -> none  [on_device(): got = lax.ppermute(theirs, 'core', [(0, 1), (1, 0)])]
  transfers between devices with their start and end apart: 2 -> 2, of which waited for: 2 -> 2; matrix products, arithmetic and copies ran while one was open for 0% -> 0% of each run, Pallas kernels for 0% -> 13%
where the time goes in v2:
time: 85.4 us; the launch traced here: 84.9 us
  blocking collectives  32.5 us (38%)
  starting transfers between devices  24 us (28%)
  Pallas kernels  14.3 us (17%)
  waiting for transfers between devices  9.63 us (11%)
  local copies, waits for them, and re-layouts  2.14 us (3%)
  between operations  1.51 us (2%)
  other arithmetic  0.91 us (1%)
    all_to_all x2, starting transfers between devices, exchanged(): return lax.all_to_all(x, axes, 0, 0, tiled=True)  24 us
    all_to_all x1, blocking collectives, exchanged(): return lax.all_to_all(x, axes, 0, 0, tiled=True)  20 us
    all_to_all x2, waiting for transfers between devices, exchanged(): return lax.all_to_all(x, axes, 0, 0, tiled=True)  9.63 us
    all_gather x1, blocking collectives, on_device(): lax.all_gather(whole.transpose(1, 0, 2).reshape(part, width), 'core')  5.77 us
    pallas_call x1, Pallas kernels, rest_part(): call(rest_kernel, 'rest_part', 0, [wide, wide, slim, prefix_columns(0, pr...  5.52 us
    pallas_call x1, Pallas kernels, own_part(): call(own_kernel, 'own_part', 0, [wide, wide, wide, slim, slim], [columns(...  5.44 us
    all_gather x1, blocking collectives, on_device(): shared = lax.all_gather(rows.reshape(n_z * part, width), 'core')  4.35 us
    pallas_call x1, Pallas kernels, prefix_part(): pl.pallas_call(prefix_kernel, in_specs=[pl.BlockSpec(memory_space=pltpu.S...  3.32 us
  transfers between devices with their start and end apart: 2, of which 2 were waited for; matrix products, arithmetic and copies ran while one was open for 0% of the time, Pallas kernels for 13%

profile of v2, /device:TPU:1, one launch (start us, length us, event | category | flops | bytes accessed | tf_op | source)
XLA Modules:
  0.0 84.9 jit_solution(8962537585433581842)
XLA Ops:
  0.6 0.7 broadcast_select_fusion
  1.4 0.7 broadcast_in_dim.4
  2.1 15.7 %all-to-all-start = ((bf16[12,16,512]{2,1,0:T(8,128)(2,1)}), bf16[12,16,512]{2,1,0:T(8,128)(2,1)S(1)}, u32[]{:S(2)}, u32[]{:S(2)}) async-start(bf16[12,16,512]{2,1,0:T(8,128)(2,1)} %broadcast_in_dim.4), calls=%async_computation | async-start | bytes 393216 | tf_op jit(solution)/shard_map/all_to_all | solution.py:218
  17.8 0.0 copy-start
  17.8 0.0 copy-start.1
  18.6 5.4 %own_part.1 = (f32[128,4096]{1,0:T(8,128)}, f32[128,4096]{1,0:T(8,128)}, f32[24,4096]{1,0:T(8,128)S(1)}) custom-call(bf16[128,4096]{1,0:T(8,128)(2,1)} %q_ref.5, bf16[128,4096]{1,0:T(8,128)(2,1)} %do_ref.5, bf16[128,4096]{1,0:T(8,128)(2,1)} %o_ref.1, bf16[128,512]{1,0:T(8,128)(2,1)} %k_ref.3, bf16[128,512]{1,0:T(8,128)(2,1)} %v_ref.1), custom_call_target="tpu_custom_call" | custom-call | flops 536870912 | bytes 8388608 | tf_op jit(solution)/shard_map/own_part/pallas_call | solution.py:166
  24.0 6.0 %all-to-all-done = bf16[12,16,512]{2,1,0:T(8,128)(2,1)S(1)} async-done(((bf16[12,16,512]{2,1,0:T(8,128)(2,1)}), bf16[12,16,512]{2,1,0:T(8,128)(2,1)S(1)}, u32[]{:S(2)}, u32[]{:S(2)}) %all-to-all-start) | async-done | bytes 196640 | tf_op jit(solution)/shard_map/all_to_all | solution.py:218
  30.0 4.4 %all_gather.12.shared_ref.pk_ref = bf16[2,192,512]{2,1,0:T(8,128)(2,1)S(1)} all-gather(bf16[1,192,512]{2,1,0:T(8,128)(2,1)S(1)} %bitcast.17), channel_id=1, replica_groups=mesh['x'=4,'y'=8,'core'=2,'z'=12] {'core'}, dimensions={0}, use_global_device_ids=true | all-gather | bytes 589824 | tf_op jit(solution)/shard_map/all_gather | solution.py:230
  34.4 0.0 copy-done
  34.4 0.0 copy-done.1
  34.4 3.3 %prefix_part.1 = (bf16[192,4096]{1,0:T(8,128)(2,1)}, f32[8,4096]{1,0:T(8,128)S(1)}, bf16[2,192,512]{2,1,0:T(8,128)(2,1)S(1)}) custom-call(s32[1]{0:T(128)S(6)} %copy.18.meta, bf16[128,4096]{1,0:T(8,128)(2,1)S(1)} %copy-done, bf16[128,4096]{1,0:T(8,128)(2,1)S(1)} %copy-done.1, bf16[2,192,512]{2,1,0:T(8,128)(2,1)S(1)} %all_gather.12.shared_ref.pk_ref, ...), custom_call_target="tpu_custom_call" | custom-call | flops 1073741824 | bytes 5242880 | tf_op jit(solution)/shard_map/prefix_part/pallas_call | solution.py:179
  37.7 2.4 %all-gather = bf16[4,192,512]{2,1,0:T(8,128)(2,1)S(1)} all-gather(bf16[2,192,512]{2,1,0:T(8,128)(2,1)S(1)} %get-tuple-element.19), channel_id=2, replica_groups=mesh['x'=4,'y'=8,'core'=2,'z'=12] {'core'}, dimensions={0}, use_global_device_ids=true | all-gather | bytes 1179648 | tf_op jit(solution)/shard_map/all_gather | solution.py:232
  40.1 0.1 fusion
  40.2 0.1 reshape.29
  40.3 20.0 %all_to_all.15 = bf16[48,16,128]{2,1,0:T(8,128)(2,1)S(1)} all-to-all(bf16[48,16,128]{2,1,0:T(8,128)(2,1)S(1)} %bitcast.16), channel_id=1, replica_groups=mesh['x'=4,'y'=8,'core'=2,'z'=12] {'x','z'}, dimensions={0} | all-to-all | bytes 393216 | tf_op jit(solution)/shard_map/all_to_all | solution.py:218
  60.3 0.1 reduce_sum.21
  60.3 0.7 broadcast_in_dim.5
  61.0 8.3 %all-to-all-start.2 = ((bf16[32,16,128]{2,1,0:T(8,128)(2,1)}), bf16[32,16,128]{2,1,0:T(8,128)(2,1)S(1)}, u32[]{:S(2)}, u32[]{:S(2)}) async-start(bf16[32,16,128]{2,1,0:T(8,128)(2,1)} %broadcast_in_dim.5), calls=%async_computation.2 | async-start | bytes 262144 | tf_op jit(solution)/shard_map/all_to_all | solution.py:218
  69.3 5.5 %rest_part.1 = (bf16[128,4096]{1,0:T(8,128)(2,1)}, bf16[128,512]{1,0:T(8,128)(2,1)}, bf16[128,512]{1,0:T(8,128)(2,1)}) custom-call(bf16[128,4096]{1,0:T(8,128)(2,1)S(1)} %copy-done, bf16[128,4096]{1,0:T(8,128)(2,1)S(1)} %copy-done.1, bf16[128,512]{1,0:T(8,128)(2,1)} %k_ref.3, bf16[2,192,512]{2,1,0:T(8,128)(2,1)S(1)} %all_gather.12.shared_ref.pk_ref, ...), custom_call_target="tpu_custom_call" | custom-call | flops 536870912 | bytes 9437184 | tf_op jit(solution)/shard_map/rest_part/pallas_call | solution.py:201
  74.8 3.6 %all-to-all-done.2 = bf16[32,16,128]{2,1,0:T(8,128)(2,1)S(1)} async-done(((bf16[32,16,128]{2,1,0:T(8,128)(2,1)}), bf16[32,16,128]{2,1,0:T(8,128)(2,1)S(1)}, u32[]{:S(2)}, u32[]{:S(2)}) %all-to-all-start.2) | async-done | bytes 131104 | tf_op jit(solution)/shard_map/all_to_all | solution.py:218
  78.5 5.8 %all_gather.15 = f32[2,16,512]{2,1,0:T(8,128)S(1)} all-gather(f32[1,16,512]{2,1,0:T(8,128)S(1)} %all_gather_reshape.7), channel_id=1, replica_groups=mesh['x'=4,'y'=8,'core'=2,'z'=12] {'core'}, dimensions={0}, use_global_device_ids=true | all-gather | bytes 98304 | tf_op jit(solution)/shard_map/all_gather | solution.py:245
  84.3 0.6 slice_bitcast_fusion
  (4 shorter events, 0.1 us)
Async XLA Ops:
  2.1 28.0 %all-to-all-start = ((bf16[12,16,512]{2,1,0:T(8,128)(2,1)}), bf16[12,16,512]{2,1,0:T(8,128)(2,1)S(1)}, u32[]{:S(2)}, u32[]{:S(2)}) async-start(bf16[12,16,512]{2,1,0:T(8,128)(2,1)} %broadcast_in_dim.4), calls=%async_computation | async-start | bytes 393216 | tf_op jit(solution)/shard_map/all_to_all | solution.py:218
  17.8 16.6 %copy-start = (bf16[128,4096]{1,0:T(8,128)(2,1)S(1)}, bf16[128,4096]{1,0:T(8,128)(2,1)}, u32[]{:S(2)}) copy-start(bf16[128,4096]{1,0:T(8,128)(2,1)} %q_ref.5) | copy-start | bytes 3145732
  17.8 16.6 %copy-start.1 = (bf16[128,4096]{1,0:T(8,128)(2,1)S(1)}, bf16[128,4096]{1,0:T(8,128)(2,1)}, u32[]{:S(2)}) copy-start(bf16[128,4096]{1,0:T(8,128)(2,1)} %do_ref.5) | copy-start | bytes 3145732
  61.0 17.4 %all-to-all-start.2 = ((bf16[32,16,128]{2,1,0:T(8,128)(2,1)}), bf16[32,16,128]{2,1,0:T(8,128)(2,1)S(1)}, u32[]{:S(2)}, u32[]{:S(2)}) async-start(bf16[32,16,128]{2,1,0:T(8,128)(2,1)} %broadcast_in_dim.5), calls=%async_computation.2 | async-start | bytes 262144 | tf_op jit(solution)/shard_map/all_to_all | solution.py:218
